TPU v7x, 32 devices: a whole 2x2x4 slice. The times are simulated.
32 devices in a mesh: wide: 8 (over z, y), narrow: 4 (over x, core).
Axes of the slice: x: 2, y: 2, z: 4, core: 2. Of those that a mesh axis runs over, the one named last changes fastest.
Arguments:
- labels: int32 [256, 128, 128], P('narrow', 'wide'), may hold values 0 or 1
- density: float32 [256, 128, 128], P('narrow', 'wide'), may hold values from 0.9 to 1.1
- velocity: float32 [3, 256, 128, 128], P(None, 'narrow', 'wide'), may hold values from 0.05 to 0.2
- owner_map: int32 [16, 8, 8], P('narrow'), may hold values from 0 to 7, as said below
Outputs:
- moments: float32 [4, 4, 8, 40, 4096], P(None, 'narrow', 'wide')
Inputs may be any that keep to these rules, and one draw needn't show every extreme that they name: owner_map[g_x, g_y, g_z] is the wide index of the device that receives block (g_x, g_y, g_z), whose image brick lies on the device with narrow index g_x // 4 and wide index g_y; the receiver has that same narrow index. From one device's brick at most 2 blocks go to any one other receiver, and in every draw some pair has 2; one device receives at most 40 blocks, and in every draw some device receives 40.
All inputs are finite; a program needn't handle non-finite values. No bound on the sum of `labels` on one device may be relied on, other than what follows from the above.
Results may differ from a plain program's by a relative error of at most 0.00002.
Values sent between devices are 32-bit elements; how exact they have to be, the bound alone decides.
A program may use at most 192 MiB of HBM per device.

v0:
```python
import functools
import math

import jax
import jax.numpy as jnp
from jax import lax
from jax.experimental import pallas as pl
from jax.experimental.pallas import tpu as pltpu
from jax.sharding import PartitionSpec as P

BS = 16
RADIUS = 2
STEPS = 4
HALO = STEPS
GHALO = HALO + RADIUS

VELOCITIES = (
    (0, 0, 0),
    (1, 0, 0),
    (-1, 0, 0),
    (0, 1, 0),
    (0, -1, 0),
    (0, 0, 1),
    (0, 0, -1),
    (1, 1, 0),
    (-1, -1, 0),
    (1, -1, 0),
    (-1, 1, 0),
    (1, 0, 1),
    (-1, 0, -1),
    (1, 0, -1),
    (-1, 0, 1),
    (0, 1, 1),
    (0, -1, -1),
    (0, 1, -1),
    (0, -1, 1),
)
MESH = pl.DeviceIdType.MESH


def gauss_weights(radius):
    raw_values = [math.exp(-0.5 * offset * offset) for offset in range(-radius, radius + 1)]
    running = 0.0
    for element in raw_values:
        running = running + element
    return [element / running for element in raw_values]


def dot_c(direction, parts):
    running = None
    for sign, part in zip(VELOCITIES[direction], parts):
        if sign == 0:
            continue
        if running is None:
            running = part if sign > 0 else -part
        else:
            running = running + part if sign > 0 else running - part
    return running


def sums_and_differences(fields):
    sums, diffs = [], []
    mom = [None, None, None]
    rho = fields[0]
    for i in range(1, 19, 2):
        s = fields[i] + fields[i + 1]
        d = fields[i] - fields[i + 1]
        sums.append(s)
        diffs.append(d)
        rho = rho + s
        for axis_no in range(3):
            sign = VELOCITIES[i][axis_no]
            if sign != 0:
                if mom[axis_no] is None:
                    mom[axis_no] = d if sign > 0 else -d
                else:
                    mom[axis_no] = mom[axis_no] + d if sign > 0 else mom[axis_no] - d
    return rho, mom, sums, diffs


def flow_kernel(
    wide_count, narrow_count, X, Y,
    labels, density, velocity, mail_src,
    src_out,
    nat, natl, zs, gx, fld, gext, grey, fa, fb, mom, rows, mail,
    own_sem, xs_sem, xr_sem, ys_sem, yr_sem, as_sem, ar_sem, out_sem,
):
    weights = gauss_weights(RADIUS)
    XE = X + 2 * HALO
    XG = X + 2 * GHALO
    YE = Y + 2 * HALO
    R = XE // 8
    wide = lax.axis_index("wide")
    narrow = lax.axis_index("narrow")
    right = lax.rem(narrow + 1, narrow_count)
    left = lax.rem(narrow + narrow_count - 1, narrow_count)
    up = lax.rem(wide + 1, wide_count)
    down = lax.rem(wide + wide_count - 1, wide_count)

    own = [
        pltpu.make_async_copy(labels, natl.at[pl.ds(GHALO * Y, X * Y)], own_sem.at[0]),
        pltpu.make_async_copy(density, nat.at[pl.ds(0, 1), pl.ds(HALO * Y, X * Y)], own_sem.at[1]),
        pltpu.make_async_copy(velocity, nat.at[pl.ds(1, 3), pl.ds(HALO * Y, X * Y)], own_sem.at[2]),
    ]
    for copy in own:
        copy.start()

    barrier = pltpu.get_barrier_semaphore()
    for target in (left, right):
        pl.semaphore_signal(barrier, inc=1, device_id=(wide, target), device_id_type=MESH)
    for offset in range(1, wide_count):
        pl.semaphore_signal(
            barrier, inc=1, device_id=(lax.rem(wide + offset, wide_count), narrow),
            device_id_type=MESH,
        )
    pl.semaphore_wait(barrier, 2 + wide_count - 1)

    def to_narrow(src, dst, k, target):
        return pltpu.make_async_remote_copy(
            src_ref=src, dst_ref=dst, send_sem=xs_sem.at[k], recv_sem=xr_sem.at[k],
            device_id=(wide, target), device_id_type=MESH,
        )

    xsends = []
    for k, (target, at, to_g, to_f) in enumerate(
        ((right, X, 0, 0), (left, None, X + GHALO, X + HALO))
    ):
        g_at = (X - GHALO) * Y if at is not None else 0
        f_at = (X - HALO) * Y if at is not None else 0
        xsends.append(to_narrow(labels.at[pl.ds(g_at, GHALO * Y)],
                                natl.at[pl.ds(to_g * Y, GHALO * Y)], 3 * k, target))
        xsends.append(to_narrow(density.at[:, pl.ds(f_at, HALO * Y)],
                                nat.at[pl.ds(0, 1), pl.ds(to_f * Y, HALO * Y)], 3 * k + 1, target))
        xsends.append(to_narrow(velocity.at[:, pl.ds(f_at, HALO * Y)],
                                nat.at[pl.ds(1, 3), pl.ds(to_f * Y, HALO * Y)], 3 * k + 2, target))
    for copy in xsends:
        copy.start()

    own[0].wait()
    xsends[0].wait_recv()
    xsends[3].wait_recv()

    def smooth_z(x, carry):
        at = pl.ds(pl.multiple_of(x * Y, 8), Y)
        v = natl[at, :].astype(jnp.float32)
        total = weights[RADIUS] * v
        for k in range(1, RADIUS + 1):
            total = total + weights[RADIUS + k] * (
                pltpu.roll(v, k, 1) + pltpu.roll(v, v.shape[1] - k, 1))
        zs[at, :] = total
        return carry

    lax.fori_loop(0, XG, smooth_z, 0)

    def smooth_x(x, carry):
        total = None
        for k in range(2 * RADIUS + 1):
            term = weights[k] * zs[pl.ds(pl.multiple_of((x + k) * Y, 8), Y), :]
            total = term if total is None else total + term
        gx[pl.ds(pl.multiple_of(x * Y, 8), Y), :] = total
        return carry

    lax.fori_loop(0, XE, smooth_x, 0)

    def fold_g(y, carry):
        for r in range(R):
            gext[GHALO + y, pl.ds(8 * r, 8), :] = gx[pl.ds(r * Y + y, 8, stride=R * Y), :]
        return carry

    lax.fori_loop(0, Y, fold_g, 0)

    def to_wide(src, dst, k, target):
        return pltpu.make_async_remote_copy(
            src_ref=src, dst_ref=dst, send_sem=ys_sem.at[k], recv_sem=yr_sem.at[k],
            device_id=(target, narrow), device_id_type=MESH,
        )

    ysends = [
        to_wide(gext.at[pl.ds(Y, GHALO)], gext.at[pl.ds(0, GHALO)], 0, up),
        to_wide(gext.at[pl.ds(GHALO, GHALO)], gext.at[pl.ds(Y + GHALO, GHALO)], 1, down),
        to_wide(fld.at[:, pl.ds(Y, HALO)], fld.at[:, pl.ds(0, HALO)], 2, up),
        to_wide(fld.at[:, pl.ds(HALO, HALO)], fld.at[:, pl.ds(Y + HALO, HALO)], 3, down),
    ]
    ysends[0].start()
    ysends[1].start()

    own[1].wait()
    own[2].wait()
    for k in (1, 2, 4, 5):
        xsends[k].wait_recv()

    def fold_f(y, carry):
        for q in range(4):
            for r in range(R):
                fld[q, HALO + y, pl.ds(8 * r, 8), :] = nat[q, pl.ds(r * Y + y, 8, stride=R * Y), :]
        return carry

    lax.fori_loop(0, Y, fold_f, 0)
    ysends[2].start()
    ysends[3].start()

    def over_rows(spans, row_fn):
        (first, last) = spans[0]
        if len(spans) == 1:
            lax.fori_loop(first, last, lambda y, c: (row_fn(y), c)[1], 0)
        else:
            gap = spans[1][0] - last

            def step(i, c):
                row_fn(jnp.where(i < last, i, i + gap))
                return c

            lax.fori_loop(first, last + spans[1][1] - spans[1][0], step, 0)

    def first_row(y):
        for r in range(R):
            at = pl.ds(8 * r, 8)
            g = weights[RADIUS] * gext[y + RADIUS, at, :]
            for k in range(1, RADIUS + 1):
                g = g + weights[RADIUS + k] * (
                    gext[y + RADIUS - k, at, :] + gext[y + RADIUS + k, at, :])
            grey[y, at, :] = g
            rho = fld[0, y, at, :]
            u = [fld[1 + n, y, at, :] for n in range(3)]
            v = [1.5 * part for part in u]
            rho12 = rho * (1.0 / 12.0)
            j = [rho12 * part for part in u]
            flip = 1.0 - 2.0 * g
            w = [flip * part for part in j]
            usq = u[0] * v[0] + u[1] * v[1] + u[2] * v[2]
            base = (rho * (1.0 / 36.0)) * (1.0 - usq)
            fa[0, y, at, :] = 12.0 * base
            base2 = base + base
            for i in range(1, 19, 2):
                even = dot_c(i, j) * dot_c(i, v)
                odd = dot_c(i, w)
                if i < 7:
                    even = base2 + (even + even)
                    odd = odd + odd
                else:
                    even = base + even
                fa[i, y, at, :] = even + odd
                fa[i + 1, y, at, :] = even - odd

    def pulled(old, y, r):
        fields = []
        for cx, cy, cz in VELOCITIES:
            i = len(fields)
            rr = r - cx
            turn = 0
            if rr < 0:
                rr, turn = R - 1, 1
            elif rr == R:
                rr, turn = 0, 7
            f = old[i, y - cy, pl.ds(8 * rr, 8), :]
            if turn:
                f = pltpu.roll(f, turn, 0)
            if cz:
                f = pltpu.roll(f, cz % f.shape[1], 1)
            fields.append(f)
        return fields

    def collide_row(old, new, y):
        for r in range(R):
            at = pl.ds(8 * r, 8)
            fields = pulled(old, y, r)
            rho, m, sums, diffs = sums_and_differences(fields)
            g = grey[y, at, :]
            om = 1.0 - g
            b = 1.25 * om
            a = -0.25 * om
            apg = a + g
            ca = 0.5 * apg
            cb = 0.5 * (a - g)
            inv = 1.5 / rho
            v = [inv * part for part in m]
            b12 = b * (1.0 / 12.0)
            j = [b12 * part for part in m]
            vsq = v[0] * v[0] + v[1] * v[1] + v[2] * v[2]
            base = ((b * (1.0 / 36.0)) * rho) * (1.0 - (2.0 / 3.0) * vsq)
            new[0, y, at, :] = apg * fields[0] + 12.0 * base
            base2 = base + base
            for p, i in enumerate(range(1, 19, 2)):
                odd = dot_c(i, j)
                even = odd * dot_c(i, v)
                if i < 7:
                    even = base2 + (even + even)
                    odd = odd + odd
                else:
                    even = base + even
                even = ca * sums[p] + even
                odd = cb * diffs[p] + odd
                new[i, y, at, :] = even + odd
                new[i + 1, y, at, :] = even - odd

    def final_row(old, y):
        for r in range(R):
            rho, m, _, _ = sums_and_differences(pulled(old, y, r))
            at = pl.ds(r * Y + y - HALO, 8, stride=R * Y)
            mom[0, at, :] = rho
            for n in range(3):
                mom[1 + n, at, :] = m[n]

    bufs = (fa, fb)
    over_rows([(HALO + RADIUS, Y + HALO - RADIUS)], first_row)
    for t in range(1, STEPS):
        over_rows(
            [(HALO + RADIUS + t, Y + HALO - RADIUS - t)],
            functools.partial(collide_row, bufs[(t - 1) % 2], bufs[t % 2]),
        )
    for copy in ysends:
        copy.wait_recv()
    over_rows([(0, HALO + RADIUS), (YE - HALO - RADIUS, YE)], first_row)
    for t in range(1, STEPS):
        over_rows(
            [(t, HALO + RADIUS + t), (YE - HALO - RADIUS - t, YE - t)],
            functools.partial(collide_row, bufs[(t - 1) % 2], bufs[t % 2]),
        )
    over_rows([(HALO, Y + HALO)], functools.partial(final_row, bufs[(STEPS - 1) % 2]))

    sub = lax.broadcasted_iota(jnp.int32, (8, 128), 0)
    grp = lax.broadcasted_iota(jnp.int32, (8, 128), 1) // BS
    same = [((sub // b) % 2) == ((grp // b) % 2) for b in (1, 2, 4)]
    low = [((sub // b) % 2) == 0 for b in (1, 2, 4)]

    def swap(v):
        for n, b in enumerate((1, 2, 4)):
            ahead = pltpu.roll(pltpu.roll(v, 8 - b, 0), BS * b, 1)
            if b == 4:
                other = ahead
            else:
                back = pltpu.roll(pltpu.roll(v, b, 0), 128 - BS * b, 1)
                other = jnp.where(low[n], ahead, back)
            v = jnp.where(same[n], v, other)
        return v

    halves = Y // 8
    chunks = BS * halves

    def to_rows(a, carry):
        for bx in range(X // BS):
            for h in range(halves):
                for q in range(4):
                    v = mom[q, pl.ds(pl.multiple_of((HALO + bx * BS + a) * Y + 8 * h, 8), 8), :]
                    rows[pl.ds(8 * bx * 4 * chunks + q * chunks + a * halves + h, 8,
                               stride=4 * chunks), :] = swap(v)
        return carry

    lax.fori_loop(0, BS, to_rows, 0)

    per = 4 * chunks
    blocks = (X // BS) * 8
    keep = pltpu.make_async_copy(rows, src_out.at[pl.ds(0, blocks * per)], out_sem)
    keep.start()
    sends = []
    for offset in range(1, wide_count):
        target = lax.rem(wide + offset, wide_count)
        for k in range(2):
            j = mail_src[target * 2 + k]
            mail[pl.ds((2 * offset + k) * per, per), :] = rows[pl.ds(j * per, per), :]
        copy = pltpu.make_async_remote_copy(
            src_ref=mail.at[pl.ds(2 * offset * per, 2 * per)],
            dst_ref=src_out.at[pl.ds((blocks + 2 * wide) * per, 2 * per)],
            send_sem=as_sem.at[offset - 1], recv_sem=ar_sem.at[offset - 1],
            device_id=(target, narrow), device_id_type=MESH,
        )
        copy.start()
        sends.append(copy)
    for copy in xsends + ysends:
        copy.wait_send()
    keep.wait()
    for copy in sends:
        copy.wait()


def collect_kernel(rows_of, src, out):
    per = 4 * out.shape[2] // 8
    count = src.shape[0] // per
    chunks = out.shape[2] // 8

    def group(sg, carry):
        for si in range(8):
            row = rows_of[sg * 8 + si]
            there = row < count
            at = jnp.minimum(row, count - 1) * per
            for q in range(4):
                for k in range(chunks // 8):
                    v = src[pl.ds(pl.multiple_of(at + q * chunks + 8 * k, 8), 8), :]
                    out[q, sg, pl.ds(64 * k + si, 8, stride=8), :] = jnp.where(there, v, 0.0)
        return carry

    lax.fori_loop(0, out.shape[1], group, 0)


def routing(owner_map, my_index):
    blocks_x, wide_count, blocks_z = owner_map.shape
    block_count = blocks_x * blocks_z
    capacity = block_count + 2 * (wide_count - 1) - 2 * ((wide_count - 1) // 2)
    places = jnp.arange(block_count, dtype=jnp.int32)
    mine = lax.dynamic_index_in_dim(owner_map, my_index, 1, keepdims=False).reshape(block_count)
    rank = jnp.sum(
        (mine[:, None] == mine[None, :]) & (places[None, :] < places[:, None]), axis=1)
    slots = jnp.arange(2 * wide_count, dtype=jnp.int32)
    mail_src = jnp.sum(
        jnp.where((mine * 2 + rank)[None, :] == slots[:, None], places[None, :], 0)
        * (rank < 2)[None, :].astype(jnp.int32), axis=1)
    mail_src = jnp.minimum(mail_src, block_count - 1)
    here = (owner_map == my_index).astype(jnp.int32)
    counts = jnp.sum(here, axis=(0, 2))
    homes = slots // 2
    from_mail = (counts[homes] > slots % 2) & (homes != my_index)
    flags = jnp.concatenate([mine == my_index, from_mail])
    order = jnp.arange(flags.shape[0], dtype=jnp.int32)
    position = jnp.sum(flags[None, :] & (order[None, :] < order[:, None]), axis=1)
    wanted = jnp.arange(capacity, dtype=jnp.int32)
    hit = flags[None, :] & (position[None, :] == wanted[:, None])
    rows_of = jnp.sum(jnp.where(hit, order[None, :] + 1, 0), axis=1) - 1
    rows_of = jnp.where(rows_of < 0, flags.shape[0], rows_of)
    return mail_src.astype(jnp.int32), rows_of.astype(jnp.int32), capacity


def body(wide_count, narrow_count, labels, density, velocity, owner_map):
    X, Y, Z = labels.shape
    my_index = lax.axis_index("wide")
    mail_src, rows_of, capacity = routing(owner_map, my_index)
    XE, YE = X + 2 * HALO, Y + 2 * HALO
    XG, YG = X + 2 * GHALO, Y + 2 * GHALO
    blocks = (X // BS) * (Z // BS)
    chunks = BS * BS * BS // 128
    per = 4 * chunks
    f32 = jnp.float32
    hbm = pl.BlockSpec(memory_space=pl.ANY)
    src = pl.pallas_call(
        functools.partial(flow_kernel, wide_count, narrow_count, X, Y),
        out_shape=jax.ShapeDtypeStruct(((blocks + 2 * wide_count) * per, Z), f32),
        in_specs=[hbm, hbm, hbm, pl.BlockSpec(memory_space=pltpu.SMEM)],
        out_specs=hbm,
        scratch_shapes=[
            pltpu.VMEM((4, XE * Y, Z), f32),
            pltpu.VMEM((XG * Y, Z), jnp.int32),
            pltpu.VMEM((XG * Y, Z), f32),
            pltpu.VMEM((XE * Y, Z), f32),
            pltpu.VMEM((4, YE, XE, Z), f32),
            pltpu.VMEM((YG, XE, Z), f32),
            pltpu.VMEM((YE, XE, Z), f32),
            pltpu.VMEM((19, YE, XE, Z), f32),
            pltpu.VMEM((19, YE, XE, Z), f32),
            pltpu.VMEM((4, XE * Y, Z), f32),
            pltpu.VMEM((blocks * per, Z), f32),
            pltpu.VMEM((2 * wide_count * per, Z), f32),
            pltpu.SemaphoreType.DMA((3,)),
            pltpu.SemaphoreType.DMA((6,)),
            pltpu.SemaphoreType.DMA((6,)),
            pltpu.SemaphoreType.DMA((4,)),
            pltpu.SemaphoreType.DMA((4,)),
            pltpu.SemaphoreType.DMA((wide_count - 1,)),
            pltpu.SemaphoreType.DMA((wide_count - 1,)),
            pltpu.SemaphoreType.DMA,
        ],
        compiler_params=pltpu.CompilerParams(
            collective_id=0, has_side_effects=True, vmem_limit_bytes=60 * 1024 * 1024
        ),
        name="flow",
    )(labels.reshape(X * Y, Z), density.reshape(1, X * Y, Z), velocity.reshape(3, X * Y, Z), mail_src)
    groups = capacity // 8
    out = pl.pallas_call(
        collect_kernel,
        out_shape=jax.ShapeDtypeStruct((4, groups, chunks * 8, Z), f32),
        in_specs=[
            pl.BlockSpec(memory_space=pltpu.SMEM),
            pl.BlockSpec(memory_space=pltpu.VMEM),
        ],
        out_specs=pl.BlockSpec(memory_space=pltpu.VMEM),
        compiler_params=pltpu.CompilerParams(vmem_limit_bytes=48 * 1024 * 1024),
        name="collect",
    )(rows_of, src)
    out = out.reshape(4, groups, chunks, 8, Z).transpose(0, 1, 3, 2, 4)
    return out.reshape(4, 1, 1, capacity, BS * BS * BS)


def solution(mesh):
    placed = (
        P("narrow", "wide", None),
        P("narrow", "wide", None),
        P(None, "narrow", "wide", None),
        P("narrow", None, None),
    )
    return jax.shard_map(
        functools.partial(body, mesh.shape["wide"], mesh.shape["narrow"]),
        mesh=mesh,
        in_specs=placed,
        out_specs=P(None, "narrow", "wide", None, None),
        check_vma=False,
    )
```

profile of v0, /device:TPU:28, one launch (start us, length us, event | category | flops | bytes accessed | tf_op | source)
XLA Modules:
  0.0 105.0 jit_solution(6586664535913325050)
XLA Ops:
  0.0 0.8 convert_reduce_fusion.2
  0.9 0.7 dynamic-slice_reduce_fusion
  1.6 0.1 reshape.86
  1.7 0.2 convert_reduce_fusion.1
  1.9 0.1 multiply_reduce_fusion
  2.0 0.5 broadcast_minimum_fusion.mail_src
  2.5 0.7 gather_fusion
  3.2 0.1 pad_add_fusion
  3.3 0.1 convert_reduce_fusion
  3.4 0.1 select_reduce_fusion
  3.5 96.9 %flow.1.src = f32[6144,128]{1,0:T(8,128)} custom-call(s32[1024,128]{1,0:T(8,128)} %bitcast.11, f32[1,1024,128]{2,1,0:T(8,128)} %bitcast.12, f32[3,1024,128]{2,1,0:T(8,128)} %bitcast.10, s32[16]{0:T(128)} %broadcast_minimum_fusion.mail_src), custom_call_target="tpu_custom_call" | custom-call | tf_op jit(solution)/shard_map/flow/pallas_call | solution.py:433
  100.4 0.0 copy-start
  100.4 1.9 %copy-done = f32[6144,128]{1,0:T(8,128)S(1)} copy-done((f32[6144,128]{1,0:T(8,128)S(1)}, f32[6144,128]{1,0:T(8,128)}, u32[]{:S(2)}) %copy-start) | copy-done | bytes 3145752
  102.3 2.7 %collect.1 = f32[4,5,256,128]{3,2,1,0:T(8,128)} custom-call(s32[40]{0:T(128)S(1)} %compare_select_fusion.rows_of, f32[6144,128]{1,0:T(8,128)S(1)} %copy-done), custom_call_target="tpu_custom_call" | custom-call | tf_op jit(solution)/shard_map/collect/pallas_call | solution.py:466
  (8 shorter events, 0.0 us)
Async XLA Ops:
  100.4 1.9 %copy-start = (f32[6144,128]{1,0:T(8,128)S(1)}, f32[6144,128]{1,0:T(8,128)}, u32[]{:S(2)}) copy-start(f32[6144,128]{1,0:T(8,128)} %flow.1.src) | copy-start | bytes 9437188
where the time goes:
time: 105 us
  Pallas kernels  99.6 us (95%)
  local copies, waits for them, and re-layouts  3.37 us (3%)
  other arithmetic  2.01 us (2%)
    pallas_call x1, Pallas kernels, body(): pl.pallas_call(functools.partial(flow_kernel, wide_count, narrow_count, X...  96.9 us
    pallas_call x1, Pallas kernels, body(): pl.pallas_call(collect_kernel, out_shape=jax.ShapeDtypeStruct((4, groups,...  2.69 us

commit v1 on v0

--- a/solution.py
+++ b/solution.py
@@ -13,6 +13,8 @@
 STEPS = 4
 HALO = STEPS
 GHALO = HALO + RADIUS
+YHALO = 1
+YGHALO = YHALO + RADIUS
 
 VELOCITIES = (
     (0, 0, 0),
@@ -36,6 +38,11 @@
     (0, -1, 1),
 )
 MESH = pl.DeviceIdType.MESH
+UPWARD = [i for i in range(19) if VELOCITIES[i][1] > 0]
+DOWNWARD = [i for i in range(19) if VELOCITIES[i][1] < 0]
+ORDER = UPWARD + DOWNWARD + [i for i in range(19) if VELOCITIES[i][1] == 0]
+SLOT = [ORDER.index(i) for i in range(19)]
+CROSS = len(UPWARD)
 
 
 def gauss_weights(radius):
@@ -83,13 +90,13 @@
     labels, density, velocity, mail_src,
     src_out,
     nat, natl, zs, gx, fld, gext, grey, fa, fb, mom, rows, mail,
-    own_sem, xs_sem, xr_sem, ys_sem, yr_sem, as_sem, ar_sem, out_sem,
+    own_sem, xs_sem, xr_sem, ys_sem, yr_sem, ps_sem, pr_sem, as_sem, ar_sem, out_sem,
 ):
     weights = gauss_weights(RADIUS)
     XE = X + 2 * HALO
     XG = X + 2 * GHALO
-    YE = Y + 2 * HALO
     R = XE // 8
+    lo, hi = YHALO, YHALO + Y - 1
     wide = lax.axis_index("wide")
     narrow = lax.axis_index("narrow")
     right = lax.rem(narrow + 1, narrow_count)
@@ -136,9 +143,19 @@
     for copy in xsends:
         copy.start()
 
-    own[0].wait()
-    xsends[0].wait_recv()
-    xsends[3].wait_recv()
+    def to_wide(src, dst, sems, k, target):
+        return pltpu.make_async_remote_copy(
+            src_ref=src, dst_ref=dst, send_sem=sems[0].at[k], recv_sem=sems[1].at[k],
+            device_id=(target, narrow), device_id_type=MESH,
+        )
+
+    ysem = (ys_sem, yr_sem)
+    ysends = [
+        to_wide(fld.at[:, pl.ds(Y, YHALO)], fld.at[:, pl.ds(0, YHALO)], ysem, 0, up),
+        to_wide(fld.at[:, pl.ds(lo, YHALO)], fld.at[:, pl.ds(Y + YHALO, YHALO)], ysem, 1, down),
+        to_wide(gext.at[pl.ds(Y, YGHALO)], gext.at[pl.ds(0, YGHALO)], ysem, 2, up),
+        to_wide(gext.at[pl.ds(YGHALO, YGHALO)], gext.at[pl.ds(Y + YGHALO, YGHALO)], ysem, 3, down),
+    ]
 
     def smooth_z(x, carry):
         at = pl.ds(pl.multiple_of(x * Y, 8), Y)
@@ -150,8 +167,6 @@
         zs[at, :] = total
         return carry
 
-    lax.fori_loop(0, XG, smooth_z, 0)
-
     def smooth_x(x, carry):
         total = None
         for k in range(2 * RADIUS + 1):
@@ -160,44 +175,36 @@
         gx[pl.ds(pl.multiple_of(x * Y, 8), Y), :] = total
         return carry
 
-    lax.fori_loop(0, XE, smooth_x, 0)
-
     def fold_g(y, carry):
         for r in range(R):
-            gext[GHALO + y, pl.ds(8 * r, 8), :] = gx[pl.ds(r * Y + y, 8, stride=R * Y), :]
+            gext[YGHALO + y, pl.ds(8 * r, 8), :] = gx[pl.ds(r * Y + y, 8, stride=R * Y), :]
         return carry
 
-    lax.fori_loop(0, Y, fold_g, 0)
-
-    def to_wide(src, dst, k, target):
-        return pltpu.make_async_remote_copy(
-            src_ref=src, dst_ref=dst, send_sem=ys_sem.at[k], recv_sem=yr_sem.at[k],
-            device_id=(target, narrow), device_id_type=MESH,
-        )
-
-    ysends = [
-        to_wide(gext.at[pl.ds(Y, GHALO)], gext.at[pl.ds(0, GHALO)], 0, up),
-        to_wide(gext.at[pl.ds(GHALO, GHALO)], gext.at[pl.ds(Y + GHALO, GHALO)], 1, down),
-        to_wide(fld.at[:, pl.ds(Y, HALO)], fld.at[:, pl.ds(0, HALO)], 2, up),
-        to_wide(fld.at[:, pl.ds(HALO, HALO)], fld.at[:, pl.ds(Y + HALO, HALO)], 3, down),
-    ]
-    ysends[0].start()
-    ysends[1].start()
-
+    def fold_f(y, carry):
+        for q in range(4):
+            for r in range(R):
+                fld[q, lo + y, pl.ds(8 * r, 8), :] = nat[q, pl.ds(r * Y + y, 8, stride=R * Y), :]
+        return carry
+
+    own[0].wait()
+    lax.fori_loop(GHALO, GHALO + X, smooth_z, 0)
     own[1].wait()
     own[2].wait()
     for k in (1, 2, 4, 5):
         xsends[k].wait_recv()
-
-    def fold_f(y, carry):
-        for q in range(4):
-            for r in range(R):
-                fld[q, HALO + y, pl.ds(8 * r, 8), :] = nat[q, pl.ds(r * Y + y, 8, stride=R * Y), :]
-        return carry
-
-    lax.fori_loop(0, Y, fold_f, 0)
+    fold_f(0, 0)
+    fold_f(Y - 1, 0)
+    ysends[0].start()
+    ysends[1].start()
+    xsends[0].wait_recv()
+    xsends[3].wait_recv()
+    lax.fori_loop(0, GHALO, smooth_z, 0)
+    lax.fori_loop(GHALO + X, XG, smooth_z, 0)
+    lax.fori_loop(0, XE, smooth_x, 0)
+    lax.fori_loop(0, Y, fold_g, 0)
     ysends[2].start()
     ysends[3].start()
+    lax.fori_loop(1, Y - 1, fold_f, 0)
 
     def over_rows(spans, row_fn):
         (first, last) = spans[0]
@@ -229,7 +236,7 @@
             w = [flip * part for part in j]
             usq = u[0] * v[0] + u[1] * v[1] + u[2] * v[2]
             base = (rho * (1.0 / 36.0)) * (1.0 - usq)
-            fa[0, y, at, :] = 12.0 * base
+            fa[SLOT[0], y, at, :] = 12.0 * base
             base2 = base + base
             for i in range(1, 19, 2):
                 even = dot_c(i, j) * dot_c(i, v)
@@ -239,8 +246,8 @@
                     odd = odd + odd
                 else:
                     even = base + even
-                fa[i, y, at, :] = even + odd
-                fa[i + 1, y, at, :] = even - odd
+                fa[SLOT[i], y, at, :] = even + odd
+                fa[SLOT[i + 1], y, at, :] = even - odd
 
     def pulled(old, y, r):
         fields = []
@@ -252,7 +259,7 @@
                 rr, turn = R - 1, 1
             elif rr == R:
                 rr, turn = 0, 7
-            f = old[i, y - cy, pl.ds(8 * rr, 8), :]
+            f = old[SLOT[i], y - cy, pl.ds(8 * rr, 8), :]
             if turn:
                 f = pltpu.roll(f, turn, 0)
             if cz:
@@ -278,7 +285,7 @@
             j = [b12 * part for part in m]
             vsq = v[0] * v[0] + v[1] * v[1] + v[2] * v[2]
             base = ((b * (1.0 / 36.0)) * rho) * (1.0 - (2.0 / 3.0) * vsq)
-            new[0, y, at, :] = apg * fields[0] + 12.0 * base
+            new[SLOT[0], y, at, :] = apg * fields[0] + 12.0 * base
             base2 = base + base
             for p, i in enumerate(range(1, 19, 2)):
                 odd = dot_c(i, j)
@@ -290,33 +297,53 @@
                     even = base + even
                 even = ca * sums[p] + even
                 odd = cb * diffs[p] + odd
-                new[i, y, at, :] = even + odd
-                new[i + 1, y, at, :] = even - odd
+                new[SLOT[i], y, at, :] = even + odd
+                new[SLOT[i + 1], y, at, :] = even - odd
 
     def final_row(old, y):
         for r in range(R):
             rho, m, _, _ = sums_and_differences(pulled(old, y, r))
-            at = pl.ds(r * Y + y - HALO, 8, stride=R * Y)
+            at = pl.ds(r * Y + y - lo, 8, stride=R * Y)
             mom[0, at, :] = rho
             for n in range(3):
                 mom[1 + n, at, :] = m[n]
 
-    bufs = (fa, fb)
-    over_rows([(HALO + RADIUS, Y + HALO - RADIUS)], first_row)
-    for t in range(1, STEPS):
-        over_rows(
-            [(HALO + RADIUS + t, Y + HALO - RADIUS - t)],
-            functools.partial(collide_row, bufs[(t - 1) % 2], bufs[t % 2]),
-        )
+    def trade(buf, t):
+        sem = (ps_sem, pr_sem)
+        return [
+            to_wide(buf.at[pl.ds(0, CROSS), hi], buf.at[pl.ds(0, CROSS), lo - 1], sem, 2 * t, up),
+            to_wide(buf.at[pl.ds(CROSS, CROSS), lo], buf.at[pl.ds(CROSS, CROSS), hi + 1], sem,
+                    2 * t + 1, down),
+        ]
+
+    step_a = functools.partial(collide_row, fa, fb)
+    over_rows([(lo + RADIUS, hi + 1 - RADIUS)], first_row)
+    over_rows([(lo + RADIUS + 1, hi - RADIUS)], step_a)
     for copy in ysends:
         copy.wait_recv()
-    over_rows([(0, HALO + RADIUS), (YE - HALO - RADIUS, YE)], first_row)
-    for t in range(1, STEPS):
-        over_rows(
-            [(t, HALO + RADIUS + t), (YE - HALO - RADIUS - t, YE - t)],
-            functools.partial(collide_row, bufs[(t - 1) % 2], bufs[t % 2]),
-        )
-    over_rows([(HALO, Y + HALO)], functools.partial(final_row, bufs[(STEPS - 1) % 2]))
+    over_rows([(lo - 1, lo + RADIUS), (hi + 1 - RADIUS, hi + 2)], first_row)
+    psends = []
+    for t in range(STEPS):
+        old, new = ((fa, fb), (fb, fa))[t % 2]
+        if t > 0:
+            for copy in psends[-1]:
+                copy.wait_recv()
+        if t < STEPS - 1:
+            if t > 1:
+                for copy in psends[-2]:
+                    copy.wait_send()
+            over_rows([(lo, lo + 1), (hi, hi + 1)], functools.partial(collide_row, old, new))
+            psends.append(trade(new, t))
+            for copy in psends[-1]:
+                copy.start()
+            if t == 0:
+                over_rows([(lo + 1, lo + RADIUS + 1), (hi - RADIUS, hi)], step_a)
+            if t < STEPS - 2:
+                over_rows([(lo + 1, hi)], functools.partial(collide_row, new, old))
+            else:
+                over_rows([(lo + 1, hi)], functools.partial(final_row, new))
+        else:
+            over_rows([(lo, lo + 1), (hi, hi + 1)], functools.partial(final_row, old))
 
     sub = lax.broadcasted_iota(jnp.int32, (8, 128), 0)
     grp = lax.broadcasted_iota(jnp.int32, (8, 128), 1) // BS
@@ -366,7 +393,7 @@
         )
         copy.start()
         sends.append(copy)
-    for copy in xsends + ysends:
+    for copy in xsends + ysends + psends[-2] + psends[-1]:
         copy.wait_send()
     keep.wait()
     for copy in sends:
@@ -374,19 +401,16 @@
 
 
 def collect_kernel(rows_of, src, out):
-    per = 4 * out.shape[2] // 8
-    count = src.shape[0] // per
-    chunks = out.shape[2] // 8
+    count, _, chunks, _ = src.shape
 
     def group(sg, carry):
         for si in range(8):
             row = rows_of[sg * 8 + si]
             there = row < count
-            at = jnp.minimum(row, count - 1) * per
-            for q in range(4):
-                for k in range(chunks // 8):
-                    v = src[pl.ds(pl.multiple_of(at + q * chunks + 8 * k, 8), 8), :]
-                    out[q, sg, pl.ds(64 * k + si, 8, stride=8), :] = jnp.where(there, v, 0.0)
+            at = jnp.minimum(row, count - 1)
+            for k in range(chunks // 8):
+                v = src[at, 0, pl.ds(8 * k, 8), :]
+                out[0, sg, pl.ds(64 * k + si, 8, stride=8), :] = jnp.where(there, v, 0.0)
         return carry
 
     lax.fori_loop(0, out.shape[1], group, 0)
@@ -423,8 +447,8 @@
     X, Y, Z = labels.shape
     my_index = lax.axis_index("wide")
     mail_src, rows_of, capacity = routing(owner_map, my_index)
-    XE, YE = X + 2 * HALO, Y + 2 * HALO
-    XG, YG = X + 2 * GHALO, Y + 2 * GHALO
+    XE, YE = X + 2 * HALO, Y + 2 * YHALO
+    XG, YG = X + 2 * GHALO, Y + 2 * YGHALO
     blocks = (X // BS) * (Z // BS)
     chunks = BS * BS * BS // 128
     per = 4 * chunks
@@ -453,6 +477,8 @@
             pltpu.SemaphoreType.DMA((6,)),
             pltpu.SemaphoreType.DMA((4,)),
             pltpu.SemaphoreType.DMA((4,)),
+            pltpu.SemaphoreType.DMA((2 * (STEPS - 1),)),
+            pltpu.SemaphoreType.DMA((2 * (STEPS - 1),)),
             pltpu.SemaphoreType.DMA((wide_count - 1,)),
             pltpu.SemaphoreType.DMA((wide_count - 1,)),
             pltpu.SemaphoreType.DMA,
@@ -466,14 +492,15 @@
     out = pl.pallas_call(
         collect_kernel,
         out_shape=jax.ShapeDtypeStruct((4, groups, chunks * 8, Z), f32),
+        grid=(4,),
         in_specs=[
             pl.BlockSpec(memory_space=pltpu.SMEM),
-            pl.BlockSpec(memory_space=pltpu.VMEM),
+            pl.BlockSpec((blocks + 2 * wide_count, 1, chunks, Z), lambda q: (0, q, 0, 0)),
         ],
-        out_specs=pl.BlockSpec(memory_space=pltpu.VMEM),
+        out_specs=pl.BlockSpec((1, groups, chunks * 8, Z), lambda q: (q, 0, 0, 0)),
         compiler_params=pltpu.CompilerParams(vmem_limit_bytes=48 * 1024 * 1024),
         name="collect",
-    )(rows_of, src)
+    )(rows_of, src.reshape(blocks + 2 * wide_count, 4, chunks, Z))
     out = out.reshape(4, groups, chunks, 8, Z).transpose(0, 1, 3, 2, 4)
     return out.reshape(4, 1, 1, capacity, BS * BS * BS)
 

time: 105 us -> 93.4 us (0.89)
  Pallas kernels: 99.6 us -> 87.6 us
    pallas_call x1, Pallas kernels: 96.9 us -> 84.6 us  [body(): pl.pallas_call(functools.partial(flow_kernel, wide_count, narrow_count, X...]
where the time goes in v1:
time: 93.4 us; the launch traced here: 93 us
  Pallas kernels  87.6 us (94%)
  local copies, waits for them, and re-layouts  3.37 us (4%)
  other arithmetic  2.01 us (2%)
    pallas_call x1, Pallas kernels, body(): pl.pallas_call(functools.partial(flow_kernel, wide_count, narrow_count, X...  84.6 us
    pallas_call x1, Pallas kernels, body(): pl.pallas_call(collect_kernel, out_shape=jax.ShapeDtypeStruct((4, groups,...  2.98 us
    unnamed x2, local copies, waits for them, and re-layouts  1.88 us

profile of v1, /device:TPU:28, one launch (start us, length us, event | category | flops | bytes accessed | tf_op | source)
XLA Modules:
  0.0 93.0 jit_solution(13268095746716420004)
XLA Ops:
  0.0 0.8 convert_reduce_fusion.2
  0.9 0.7 dynamic-slice_reduce_fusion
  1.6 0.1 reshape.89
  1.7 0.2 convert_reduce_fusion.1
  1.9 0.1 multiply_reduce_fusion
  2.0 0.5 broadcast_minimum_fusion.mail_src
  2.5 0.7 gather_fusion
  3.2 0.1 pad_add_fusion
  3.3 0.1 convert_reduce_fusion
  3.4 0.1 select_reduce_fusion
  3.5 84.6 %flow.1 = f32[6144,128]{1,0:T(8,128)} custom-call(s32[1024,128]{1,0:T(8,128)} %bitcast.13, f32[1,1024,128]{2,1,0:T(8,128)} %bitcast.14, f32[3,1024,128]{2,1,0:T(8,128)} %bitcast.12, s32[16]{0:T(128)} %broadcast_minimum_fusion.mail_src), custom_call_target="tpu_custom_call" | custom-call | tf_op jit(solution)/shard_map/flow/pallas_call | solution.py:457
  88.2 0.0 copy-start
  88.2 1.9 %copy-done = f32[6144,128]{1,0:T(8,128)S(1)} copy-done((f32[6144,128]{1,0:T(8,128)S(1)}, f32[6144,128]{1,0:T(8,128)}, u32[]{:S(2)}) %copy-start) | copy-done | bytes 3145752
  90.1 3.0 %collect.1 = f32[4,5,256,128]{3,2,1,0:T(8,128)} custom-call(s32[40]{0:T(128)S(1)} %compare_select_fusion.rows_of, f32[48,4,32,128]{3,2,1,0:T(8,128)S(1)} %bitcast.11), custom_call_target="tpu_custom_call" | custom-call | tf_op jit(solution)/shard_map/collect/pallas_call | solution.py:492
  (8 shorter events, 0.0 us)
Async XLA Ops:
  88.2 1.9 %copy-start = (f32[6144,128]{1,0:T(8,128)S(1)}, f32[6144,128]{1,0:T(8,128)}, u32[]{:S(2)}) copy-start(f32[6144,128]{1,0:T(8,128)} %flow.1) | copy-start | bytes 9437188

commit v2 on v1

--- a/solution.py
+++ b/solution.py
@@ -157,23 +157,28 @@
         to_wide(gext.at[pl.ds(YGHALO, YGHALO)], gext.at[pl.ds(Y + YGHALO, YGHALO)], ysem, 3, down),
     ]
 
-    def smooth_z(x, carry):
-        at = pl.ds(pl.multiple_of(x * Y, 8), Y)
+    def smooth_z(x, count):
+        at = pl.ds(pl.multiple_of(x * Y, 8), count * Y)
         v = natl[at, :].astype(jnp.float32)
         total = weights[RADIUS] * v
         for k in range(1, RADIUS + 1):
             total = total + weights[RADIUS + k] * (
                 pltpu.roll(v, k, 1) + pltpu.roll(v, v.shape[1] - k, 1))
         zs[at, :] = total
-        return carry
-
-    def smooth_x(x, carry):
+
+    def smooth_x(x, count):
         total = None
         for k in range(2 * RADIUS + 1):
-            term = weights[k] * zs[pl.ds(pl.multiple_of((x + k) * Y, 8), Y), :]
+            term = weights[k] * zs[pl.ds(pl.multiple_of((x + k) * Y, 8), count * Y), :]
             total = term if total is None else total + term
-        gx[pl.ds(pl.multiple_of(x * Y, 8), Y), :] = total
-        return carry
+        gx[pl.ds(pl.multiple_of(x * Y, 8), count * Y), :] = total
+
+    def in_chunks(fn, first, count, size):
+        def step(n, carry):
+            fn(first + n * size, size)
+            return carry
+
+        lax.fori_loop(0, count // size, step, 0)
 
     def fold_g(y, carry):
         for r in range(R):
@@ -187,7 +192,7 @@
         return carry
 
     own[0].wait()
-    lax.fori_loop(GHALO, GHALO + X, smooth_z, 0)
+    in_chunks(smooth_z, GHALO, X, 8)
     own[1].wait()
     own[2].wait()
     for k in (1, 2, 4, 5):
@@ -198,9 +203,9 @@
     ysends[1].start()
     xsends[0].wait_recv()
     xsends[3].wait_recv()
-    lax.fori_loop(0, GHALO, smooth_z, 0)
-    lax.fori_loop(GHALO + X, XG, smooth_z, 0)
-    lax.fori_loop(0, XE, smooth_x, 0)
+    smooth_z(0, GHALO)
+    smooth_z(GHALO + X, GHALO)
+    in_chunks(smooth_x, 0, XE, 4)
     lax.fori_loop(0, Y, fold_g, 0)
     ysends[2].start()
     ysends[3].start()
@@ -364,35 +369,41 @@
     halves = Y // 8
     chunks = BS * halves
 
+    per = 4 * chunks
+    blocks = (X // BS) * 8
+    half = per // 2
+    quarter = chunks // 2
+
     def to_rows(a, carry):
+        part = a // (BS // 2)
+        base = part * half + (a - part * (BS // 2)) * halves
         for bx in range(X // BS):
             for h in range(halves):
                 for q in range(4):
                     v = mom[q, pl.ds(pl.multiple_of((HALO + bx * BS + a) * Y + 8 * h, 8), 8), :]
-                    rows[pl.ds(8 * bx * 4 * chunks + q * chunks + a * halves + h, 8,
-                               stride=4 * chunks), :] = swap(v)
+                    rows[pl.ds(8 * bx * per + base + q * quarter + h, 8, stride=per), :] = swap(v)
         return carry
 
-    lax.fori_loop(0, BS, to_rows, 0)
-
-    per = 4 * chunks
-    blocks = (X // BS) * 8
+    sends = []
+    for part in range(2):
+        lax.fori_loop(part * (BS // 2), (part + 1) * (BS // 2), to_rows, 0)
+        for offset in range(1, wide_count):
+            target = lax.rem(wide + offset, wide_count)
+            for k in range(2):
+                j = mail_src[target * 2 + k]
+                here = pl.ds((2 * offset + k) * per + part * half, half)
+                mail[here, :] = rows[pl.ds(j * per + part * half, half), :]
+                n = 4 * (offset - 1) + 2 * part + k
+                copy = pltpu.make_async_remote_copy(
+                    src_ref=mail.at[here],
+                    dst_ref=src_out.at[pl.ds((blocks + 2 * wide + k) * per + part * half, half)],
+                    send_sem=as_sem.at[n], recv_sem=ar_sem.at[n],
+                    device_id=(target, narrow), device_id_type=MESH,
+                )
+                copy.start()
+                sends.append(copy)
     keep = pltpu.make_async_copy(rows, src_out.at[pl.ds(0, blocks * per)], out_sem)
     keep.start()
-    sends = []
-    for offset in range(1, wide_count):
-        target = lax.rem(wide + offset, wide_count)
-        for k in range(2):
-            j = mail_src[target * 2 + k]
-            mail[pl.ds((2 * offset + k) * per, per), :] = rows[pl.ds(j * per, per), :]
-        copy = pltpu.make_async_remote_copy(
-            src_ref=mail.at[pl.ds(2 * offset * per, 2 * per)],
-            dst_ref=src_out.at[pl.ds((blocks + 2 * wide) * per, 2 * per)],
-            send_sem=as_sem.at[offset - 1], recv_sem=ar_sem.at[offset - 1],
-            device_id=(target, narrow), device_id_type=MESH,
-        )
-        copy.start()
-        sends.append(copy)
     for copy in xsends + ysends + psends[-2] + psends[-1]:
         copy.wait_send()
     keep.wait()
@@ -401,52 +412,66 @@
 
 
 def collect_kernel(rows_of, src, out):
-    count, _, chunks, _ = src.shape
+    count, _, _, quarter, _ = src.shape
 
     def group(sg, carry):
         for si in range(8):
             row = rows_of[sg * 8 + si]
             there = row < count
             at = jnp.minimum(row, count - 1)
-            for k in range(chunks // 8):
-                v = src[at, 0, pl.ds(8 * k, 8), :]
-                out[0, sg, pl.ds(64 * k + si, 8, stride=8), :] = jnp.where(there, v, 0.0)
+            for part in range(2):
+                for k in range(quarter // 8):
+                    v = src[at, part, 0, pl.ds(8 * k, 8), :]
+                    out[0, sg, pl.ds(8 * (part * quarter + 8 * k) + si, 8, stride=8), :] = (
+                        jnp.where(there, v, 0.0))
         return carry
 
     lax.fori_loop(0, out.shape[1], group, 0)
 
 
-def routing(owner_map, my_index):
-    blocks_x, wide_count, blocks_z = owner_map.shape
+def routing_kernel(capacity, owners, mail_src, rows_of, seen):
+    blocks_x, wide_count, blocks_z = owners.shape
     block_count = blocks_x * blocks_z
-    capacity = block_count + 2 * (wide_count - 1) - 2 * ((wide_count - 1) // 2)
-    places = jnp.arange(block_count, dtype=jnp.int32)
-    mine = lax.dynamic_index_in_dim(owner_map, my_index, 1, keepdims=False).reshape(block_count)
-    rank = jnp.sum(
-        (mine[:, None] == mine[None, :]) & (places[None, :] < places[:, None]), axis=1)
-    slots = jnp.arange(2 * wide_count, dtype=jnp.int32)
-    mail_src = jnp.sum(
-        jnp.where((mine * 2 + rank)[None, :] == slots[:, None], places[None, :], 0)
-        * (rank < 2)[None, :].astype(jnp.int32), axis=1)
-    mail_src = jnp.minimum(mail_src, block_count - 1)
-    here = (owner_map == my_index).astype(jnp.int32)
-    counts = jnp.sum(here, axis=(0, 2))
-    homes = slots // 2
-    from_mail = (counts[homes] > slots % 2) & (homes != my_index)
-    flags = jnp.concatenate([mine == my_index, from_mail])
-    order = jnp.arange(flags.shape[0], dtype=jnp.int32)
-    position = jnp.sum(flags[None, :] & (order[None, :] < order[:, None]), axis=1)
-    wanted = jnp.arange(capacity, dtype=jnp.int32)
-    hit = flags[None, :] & (position[None, :] == wanted[:, None])
-    rows_of = jnp.sum(jnp.where(hit, order[None, :] + 1, 0), axis=1) - 1
-    rows_of = jnp.where(rows_of < 0, flags.shape[0], rows_of)
-    return mail_src.astype(jnp.int32), rows_of.astype(jnp.int32), capacity
+    me = lax.axis_index("wide")
+
+    def clear(o, carry):
+        seen[o] = 0
+        mail_src[2 * o] = 0
+        mail_src[2 * o + 1] = 0
+        return carry
+
+    lax.fori_loop(0, wide_count, clear, 0)
+    slot = jnp.int32(0)
+    for j in range(block_count):
+        o = owners[j // blocks_z, me, j % blocks_z]
+        rank = seen[o]
+        seen[o] = rank + 1
+        mine = o == me
+        rows_of[slot] = j
+        slot = slot + jnp.where(mine, 1, 0)
+        mail_src[jnp.where(mine, 2 * wide_count, 2 * o + jnp.minimum(rank, 1))] = j
+
+    def from_home(home, slot):
+        found = jnp.int32(0)
+        for j in range(block_count):
+            found = found + jnp.where(owners[j // blocks_z, home, j % blocks_z] == me, 1, 0)
+        found = jnp.where(home == me, 0, found)
+        for k in range(2):
+            rows_of[slot] = block_count + 2 * home + k
+            slot = slot + jnp.where(found > k, 1, 0)
+        return slot
+
+    slot = lax.fori_loop(0, wide_count, from_home, slot)
+
+    def empty(s, carry):
+        rows_of[s] = jnp.where(s < slot, rows_of[s], block_count + 2 * wide_count)
+        return carry
+
+    lax.fori_loop(0, capacity, empty, 0)
 
 
 def body(wide_count, narrow_count, labels, density, velocity, owner_map):
     X, Y, Z = labels.shape
-    my_index = lax.axis_index("wide")
-    mail_src, rows_of, capacity = routing(owner_map, my_index)
     XE, YE = X + 2 * HALO, Y + 2 * YHALO
     XG, YG = X + 2 * GHALO, Y + 2 * YGHALO
     blocks = (X // BS) * (Z // BS)
@@ -454,6 +479,19 @@
     per = 4 * chunks
     f32 = jnp.float32
     hbm = pl.BlockSpec(memory_space=pl.ANY)
+    smem = pl.BlockSpec(memory_space=pltpu.SMEM)
+    capacity = blocks + 2 * (wide_count - 1) - 2 * ((wide_count - 1) // 2)
+    mail_src, rows_of = pl.pallas_call(
+        functools.partial(routing_kernel, capacity),
+        out_shape=[
+            jax.ShapeDtypeStruct((2 * wide_count + 1,), jnp.int32),
+            jax.ShapeDtypeStruct((capacity + 1,), jnp.int32),
+        ],
+        in_specs=[smem],
+        out_specs=[smem, smem],
+        scratch_shapes=[pltpu.SMEM((wide_count,), jnp.int32)],
+        name="routing",
+    )(owner_map)
     src = pl.pallas_call(
         functools.partial(flow_kernel, wide_count, narrow_count, X, Y),
         out_shape=jax.ShapeDtypeStruct(((blocks + 2 * wide_count) * per, Z), f32),
@@ -479,8 +517,8 @@
             pltpu.SemaphoreType.DMA((4,)),
             pltpu.SemaphoreType.DMA((2 * (STEPS - 1),)),
             pltpu.SemaphoreType.DMA((2 * (STEPS - 1),)),
-            pltpu.SemaphoreType.DMA((wide_count - 1,)),
-            pltpu.SemaphoreType.DMA((wide_count - 1,)),
+            pltpu.SemaphoreType.DMA((4 * (wide_count - 1),)),
+            pltpu.SemaphoreType.DMA((4 * (wide_count - 1),)),
             pltpu.SemaphoreType.DMA,
         ],
         compiler_params=pltpu.CompilerParams(
@@ -495,12 +533,12 @@
         grid=(4,),
         in_specs=[
             pl.BlockSpec(memory_space=pltpu.SMEM),
-            pl.BlockSpec((blocks + 2 * wide_count, 1, chunks, Z), lambda q: (0, q, 0, 0)),
+            pl.BlockSpec((blocks + 2 * wide_count, 2, 1, chunks // 2, Z), lambda q: (0, 0, q, 0, 0)),
         ],
         out_specs=pl.BlockSpec((1, groups, chunks * 8, Z), lambda q: (q, 0, 0, 0)),
-        compiler_params=pltpu.CompilerParams(vmem_limit_bytes=48 * 1024 * 1024),
+        compiler_params=pltpu.CompilerParams(vmem_limit_bytes=60 * 1024 * 1024),
         name="collect",
-    )(rows_of, src.reshape(blocks + 2 * wide_count, 4, chunks, Z))
+    )(rows_of, src.reshape(blocks + 2 * wide_count, 2, 4, chunks // 2, Z))
     out = out.reshape(4, groups, chunks, 8, Z).transpose(0, 1, 3, 2, 4)
     return out.reshape(4, 1, 1, capacity, BS * BS * BS)
 

time: 93.4 us -> 88.5 us (0.948)
  local copies, waits for them, and re-layouts: 3.37 us -> 0 us
  other arithmetic: 2.01 us -> 0 us
    pallas_call x1, Pallas kernels: 84.6 us -> 81.3 us  [body(): pl.pallas_call(functools.partial(flow_kernel, wide_count, narrow_count, X...]
    pallas_call x0 -> x1, Pallas kernels: none -> 2.39 us  [body(): pl.pallas_call(functools.partial(routing_kernel, capacity), out_shape=[ja...]
    unnamed x2 -> x0, local copies, waits for them, and re-layouts: 1.88 us -> none
    pallas_call x1, Pallas kernels: 2.98 us -> 4.46 us  [body(): pl.pallas_call(collect_kernel, out_shape=jax.ShapeDtypeStruct((4, groups,...]
    reduce_sum x5 -> x0, other arithmetic: 1.37 us -> none  [the longest x1 0.83 us: routing(): counts = jnp.sum(here, axis=(0, 2))]
where the time goes in v2:
time: 88.5 us; the launch traced here: 88.2 us
  Pallas kernels  88.2 us (100%)
    pallas_call x1, Pallas kernels, body(): pl.pallas_call(functools.partial(flow_kernel, wide_count, narrow_count, X...  81.3 us
    pallas_call x1, Pallas kernels, body(): pl.pallas_call(collect_kernel, out_shape=jax.ShapeDtypeStruct((4, groups,...  4.46 us
    pallas_call x1, Pallas kernels, body(): pl.pallas_call(functools.partial(routing_kernel, capacity), out_shape=[ja...  2.39 us

profile of v2, /device:TPU:28, one launch (start us, length us, event | category | flops | bytes accessed | tf_op | source)
XLA Modules:
  0.0 88.2 jit_solution(677855895729322226)
XLA Ops:
  0.0 2.4 %routing.1 = (s32[17]{0:T(128)}, s32[41]{0:T(128)}) custom-call(s32[4,8,8]{2,1,0:T(8,128)} %owners.1), custom_call_target="tpu_custom_call" | custom-call | tf_op jit(solution)/shard_map/routing/pallas_call | solution.py:484
  2.4 81.3 %flow.1 = f32[6144,128]{1,0:T(8,128)} custom-call(s32[1024,128]{1,0:T(8,128)} %bitcast.11, f32[1,1024,128]{2,1,0:T(8,128)} %bitcast.12, f32[3,1024,128]{2,1,0:T(8,128)} %bitcast.10, s32[17]{0:T(128)} %get-tuple-element.8.mail_src), custom_call_target="tpu_custom_call" | custom-call | tf_op jit(solution)/shard_map/flow/pallas_call | solution.py:495
  83.7 4.5 %collect.1 = f32[4,5,256,128]{3,2,1,0:T(8,128)} custom-call(s32[41]{0:T(128)} %get-tuple-element.7.rows_of, f32[48,2,4,16,128]{4,3,2,1,0:T(8,128)} %bitcast.9), custom_call_target="tpu_custom_call" | custom-call | tf_op jit(solution)/shard_map/collect/pallas_call | solution.py:530
